TPU v7x, 32 devices: a whole 2x2x4 slice. The times are simulated.
32 devices in a mesh: dp: 4 (over z), tensor: 8 (over y, x, core).
Axes of the slice: x: 2, y: 2, z: 4, core: 2. Of those that a mesh axis runs over, the one named last changes fastest.
Arguments:
- tokens: bfloat16 [8, 1024, 2048], P('dp', 'tensor'), may hold values from -6 to 6
- lengths: int32 [8], P('dp'), may hold values from 256 to 1024, as said below
- query_weight: bfloat16 [2048, 2048], P(None, 'tensor'), may hold values from -0.125 to 0.125
- key_weight: bfloat16 [2048, 128], replicated, may hold values from -0.125 to 0.125
- value_weight: bfloat16 [2048, 128], replicated, may hold values from -0.125 to 0.125
- output_weight: bfloat16 [2048, 2048], P('tensor'), may hold values from -2 to 2
- gate_weight: bfloat16 [2048, 5632], P(None, 'tensor'), may hold values from -0.125 to 0.125
- up_weight: bfloat16 [2048, 5632], P(None, 'tensor'), may hold values from -0.125 to 0.125
- down_weight: bfloat16 [5632, 2048], P('tensor'), may hold values from -0.078125 to 0.078125
- gain_attn: bfloat16 [2048], replicated, may hold values from 0.5 to 1.5
- gain_mlp: bfloat16 [2048], replicated, may hold values from 0.5 to 1.5
- pair_grad: float32 [4, 8, 2048, 256], P('dp', 'tensor'), may hold values from -240 to 240
- cotangent: bfloat16 [8, 1024, 2048], P('dp', 'tensor'), may hold values from -6 to 6
Outputs:
- output: bfloat16 [8, 1024, 2048], P('dp', 'tensor')
- grad_tokens: float32 [8, 1024, 2048], P('dp', 'tensor')
- grad_query: float32 [2048, 2048], P(None, 'tensor')
- grad_key: float32 [2048, 128], replicated
- grad_value: float32 [2048, 128], replicated
- output_weight_gradient: float32 [2048, 2048], P('tensor')
- grad_gate: float32 [2048, 5632], P(None, 'tensor')
- grad_up: float32 [2048, 5632], P(None, 'tensor')
- down_weight_gradient: float32 [5632, 2048], P('tensor')
- grad_gain_attn: float32 [2048], replicated
- grad_gain_mlp: float32 [2048], replicated
Inputs may be any that keep to these rules, and one draw needn't show every extreme that they name: `lengths`: in every draw at least one sequence fills its whole slot of 1024 positions.
All inputs are finite; a program needn't handle non-finite values.
Results may differ from a plain program's by a relative error of at most 0.013.
Values may be sent and summed in bfloat16 or wider, within the bound.
No kernel may reach another device: no remote copies, remote signals or barrier semaphores. Data moves between devices by JAX's collectives and lax.ppermute only.
A program may use at most 256 MiB of HBM per device.

v0:
```python
import functools

import jax
import jax.numpy as jnp
from jax import lax
from jax.experimental import pallas as pl
from jax.experimental.pallas import tpu as pltpu
from jax.sharding import PartitionSpec as P

HEAD = 128
KEY_BLOCK = 256
JOIN_COST = 8_000_000_000
BACK_COST = 1
FORTH_COST = 60
SMALL_SHIFT = 1e-05
ROPE_BASE = 10000.0
NEG_FILL = -1e30
LOG2E = 1.4426950408889634
F32 = jnp.float32
BF16 = jnp.bfloat16


def rms_scale(values):
    return lax.rsqrt(jnp.mean(values * values, axis=-1, keepdims=True) + SMALL_SHIFT)


def normed(values, gain_vec):
    return values * rms_scale(values) * gain_vec


def norm_back(values, gain_vec, grad_vals):
    scale_vals = rms_scale(values)
    scaled = grad_vals * gain_vec
    inner_mean = jnp.mean(scaled * values, axis=-1, keepdims=True)
    grad_values = scale_vals * scaled - values * (scale_vals * scale_vals * scale_vals) * inner_mean
    grad_gain = jnp.sum(grad_vals * values * scale_vals, axis=(0, 1))
    return grad_values, grad_gain


def rope_block(start, rows):
    half = HEAD // 2
    frequency = ROPE_BASE ** (-2.0 * jnp.arange(half, dtype=F32) / HEAD)
    angles = (start + jnp.arange(rows)).astype(F32)[:, None] * frequency[None, :]
    cosine, sine = jnp.cos(angles), jnp.sin(angles)
    return jnp.concatenate([cosine, cosine], 1), jnp.concatenate([-sine, sine], 1)


def swap(values, bit):
    n = lax.axis_size("tensor")
    return lax.ppermute(values, "tensor", [(i, i ^ bit) for i in range(n)])


def dot(a, b, dims, out=F32):
    return lax.dot_general(a, b, (dims, ((), ())), preferred_element_type=F32).astype(out)


def add_up(*parts):
    total = parts[0].astype(F32)
    for part in parts[1:]:
        total = total + part.astype(F32)
    return total


def key_branches(start, rows, span, body):
    blocks = span // KEY_BLOCK
    needed = (start + rows + KEY_BLOCK - 1) // KEY_BLOCK
    for count in range(1, blocks + 1):
        pl.when(needed == count)(functools.partial(body, count * KEY_BLOCK))


def stack_heads(values, heads):
    return jnp.concatenate([values[:, h * HEAD : (h + 1) * HEAD] for h in range(heads)], axis=0)


def matmul(a, b, contract):
    return lax.dot_general(a, b, (contract, ((), ())), preferred_element_type=F32)


def masked_scores(keys, query, start, rows, heads, count):
    scores = matmul(keys, query, ((1,), (1,)))
    key_pos = lax.broadcasted_iota(jnp.int32, (KEY_BLOCK, rows), 0) + (count - KEY_BLOCK)
    row_pos = lax.broadcasted_iota(jnp.int32, (KEY_BLOCK, rows), 1) + start
    allowed = key_pos <= row_pos
    last = scores[count - KEY_BLOCK :]
    last = jnp.concatenate(
        [jnp.where(allowed, last[:, h * rows : (h + 1) * rows], NEG_FILL) for h in range(heads)], axis=1
    )
    if count == KEY_BLOCK:
        return last
    return jnp.concatenate([scores[: count - KEY_BLOCK], last], axis=0)


def forward_kernel(
    place, lengths, x0_ref, x1_ref, wq_ref, kv_ref, cos_ref, sin_ref, mixed_ref, query_ref, lse_ref, raw_ref, vt_ref
):
    a, s = pl.program_id(0), pl.program_id(1)
    seqs, span = kv_ref.shape[0], kv_ref.shape[1]
    rows = x0_ref.shape[0] // seqs
    heads = wq_ref.shape[1] // HEAD
    start = place[a] * rows
    here = pl.ds(pl.multiple_of(s * rows, rows), rows)
    live = start < lengths[s]
    factor = HEAD ** (-0.5) * LOG2E

    for k, x_ref in enumerate((x0_ref, x1_ref)):

        @pl.when((a == k) & (s == 0))
        def _(x_ref=x_ref):
            raw_ref[...] = matmul(x_ref[...], wq_ref[...], ((1,), (0,)))

    @pl.when(a == 0)
    def _():
        vt_ref[s] = kv_ref[s, :, HEAD:].T

    pieces = []
    for h in range(heads):
        raw = raw_ref[here, h * HEAD : (h + 1) * HEAD]
        pieces.append((raw * cos_ref[0] + pltpu.roll(raw, HEAD // 2, 1) * sin_ref[0]).astype(BF16))
    query_ref[0, s] = jnp.concatenate(pieces, axis=0)

    def body(count):
        scores = masked_scores(kv_ref[s, :count, :HEAD], query_ref[0, s], start, rows, heads, count)
        top = jnp.max(scores, axis=0, keepdims=True)
        terms = jnp.exp2((scores - top) * factor)
        total = jnp.sum(terms, axis=0, keepdims=True)
        out = matmul(vt_ref[s, :, :count], terms.astype(BF16), ((1,), (0,))) / total
        lse_ref[0, s] = jnp.broadcast_to(top * factor + jnp.log2(total), lse_ref.shape[2:])
        for h in range(heads):
            piece = out[:, h * rows : (h + 1) * rows].T
            mixed_ref[0, here, h * HEAD : (h + 1) * HEAD] = piece.astype(BF16)

    @pl.when(live)
    def _():
        key_branches(start, rows, span, body)

    @pl.when(jnp.logical_not(live))
    def _():
        mixed_ref[0, here] = jnp.zeros((rows, heads * HEAD), BF16)
        lse_ref[0, s] = jnp.zeros(lse_ref.shape[2:], F32)


def whole(shape):
    return pl.BlockSpec(shape, lambda a, *_: (0,) * len(shape))


def blocked(shape):
    return pl.BlockSpec((1, *shape[1:]), lambda a, *_: (a,) + (0,) * (len(shape) - 1))


def attention_forward(place, lengths, parts, query_weights, kv, cosine, sine):
    flat, width = parts[0].shape
    seqs, span = kv.shape[0], kv.shape[1]
    rows, wide = flat // seqs, query_weights.shape[1]
    heads = wide // HEAD
    shapes = [(2, flat, wide), (2, seqs, heads * rows, HEAD), (2, seqs, 8, heads * rows)]
    return pl.pallas_call(
        forward_kernel,
        grid_spec=pltpu.PrefetchScalarGridSpec(
            num_scalar_prefetch=2,
            grid=(2, seqs),
            in_specs=[
                whole(parts[0].shape),
                whole(parts[1].shape),
                whole(query_weights.shape),
                whole(kv.shape),
                blocked(cosine.shape),
                blocked(sine.shape),
            ],
            out_specs=[blocked(shape) for shape in shapes],
            scratch_shapes=[pltpu.VMEM((flat, wide), F32), pltpu.VMEM((seqs, HEAD, span), BF16)],
        ),
        out_shape=[jax.ShapeDtypeStruct(s, t) for s, t in zip(shapes, (BF16, BF16, F32))],
        compiler_params=pltpu.CompilerParams(vmem_limit_bytes=48 * 1024 * 1024),
        cost_estimate=pl.CostEstimate(flops=FORTH_COST * flat * wide * span, bytes_accessed=kv.size, transcendentals=0),
        name="attention_forward",
    )(place, lengths, *parts, query_weights, kv, cosine, sine)


def backward_kernel(
    place, lengths, g0_ref, g1_ref, wo_ref, wq_ref, query_ref, lse_ref, kv_ref, cos_ref, sin_ref,
    gq_ref, in_ref, gkv_ref, gm_ref, kt_ref,
):
    a, s = pl.program_id(0), pl.program_id(1)
    seqs, span = kv_ref.shape[0], kv_ref.shape[1]
    rows = g0_ref.shape[0] // seqs
    heads = wq_ref.shape[1] // HEAD
    start = place[a] * rows
    here = pl.ds(pl.multiple_of(s * rows, rows), rows)
    live = start < lengths[s]
    scale = HEAD ** (-0.5)
    factor = scale * LOG2E

    for k, g_ref in enumerate((g0_ref, g1_ref)):

        @pl.when((a == k) & (s == 0))
        def _(g_ref=g_ref):
            gm_ref[...] = matmul(g_ref[...], wo_ref[...], ((1,), (1,))).astype(BF16)

    @pl.when(a == 0)
    def _():
        gkv_ref[s] = jnp.zeros(gkv_ref.shape[1:], F32)
        kt_ref[s] = kv_ref[s, :, :HEAD].T

    def body(count):
        query = query_ref[0, s]
        grad = stack_heads(gm_ref[here, :], heads)
        scores = masked_scores(kv_ref[s, :count, :HEAD], query, start, rows, heads, count)
        probs = jnp.exp2(scores * factor - lse_ref[0, s, 0:1, :])
        grad_probs = matmul(kv_ref[s, :count, HEAD:], grad, ((1,), (1,)))
        row_dots = jnp.sum(probs * grad_probs, axis=0, keepdims=True)
        grad_scores = (probs * (grad_probs - row_dots)).astype(BF16)
        gkv_ref[s, :count, :HEAD] += scale * matmul(grad_scores, query, ((1,), (0,)))
        gkv_ref[s, :count, HEAD:] += matmul(probs.astype(BF16), grad, ((1,), (0,)))
        grad_query = matmul(kt_ref[s, :, :count], grad_scores, ((1,), (0,)))
        for h in range(heads):
            piece = grad_query[:, h * rows : (h + 1) * rows].T * scale
            piece = piece * cos_ref[0] - pltpu.roll(piece, HEAD // 2, 1) * sin_ref[0]
            gq_ref[0, here, h * HEAD : (h + 1) * HEAD] = piece.astype(BF16)

    @pl.when(live)
    def _():
        key_branches(start, rows, span, body)

    @pl.when(jnp.logical_not(live))
    def _():
        gq_ref[0, here] = jnp.zeros((rows, heads * HEAD), BF16)

    @pl.when(s == seqs - 1)
    def _():
        in_ref[0] = matmul(gq_ref[0], wq_ref[...], ((1,), (1,))).astype(BF16)


def attention_backward(place, lengths, grads, output_weights, query_weights, query, lse, kv, cosine, sine):
    flat, width = grads[0].shape
    seqs, span = kv.shape[0], kv.shape[1]
    wide = query_weights.shape[1]
    operands = (*grads, output_weights, query_weights, query, lse, kv, cosine, sine)
    specs = [whole(v.shape) for v in operands]
    for k in (4, 5, 7, 8):
        specs[k] = blocked(operands[k].shape)
    return pl.pallas_call(
        backward_kernel,
        grid_spec=pltpu.PrefetchScalarGridSpec(
            num_scalar_prefetch=2,
            grid=(2, seqs),
            in_specs=specs,
            out_specs=[blocked((2, flat, wide)), blocked((2, flat, width)), whole(kv.shape)],
            scratch_shapes=[pltpu.VMEM((flat, wide), BF16), pltpu.VMEM((seqs, HEAD, span), BF16)],
        ),
        out_shape=[
            jax.ShapeDtypeStruct((2, flat, wide), BF16),
            jax.ShapeDtypeStruct((2, flat, width), BF16),
            jax.ShapeDtypeStruct(kv.shape, F32),
        ],
        compiler_params=pltpu.CompilerParams(vmem_limit_bytes=56 * 1024 * 1024),
        cost_estimate=pl.CostEstimate(flops=BACK_COST * flat * wide * span, bytes_accessed=kv.size, transcendentals=0),
        name="attention_backward",
    )(place, lengths, *operands)


def join_columns(parts):
    rows, wide = parts[0].shape

    def kernel(*refs):
        for k in range(len(parts)):
            refs[-1][:, k * wide : (k + 1) * wide] = refs[k][...]

    return pl.pallas_call(
        kernel,
        grid=(4,),
        in_specs=[pl.BlockSpec((rows // 4, wide), lambda i: (i, 0)) for _ in parts],
        out_specs=pl.BlockSpec((rows // 4, wide * len(parts)), lambda i: (i, 0)),
        out_shape=jax.ShapeDtypeStruct((rows, wide * len(parts)), parts[0].dtype),
        cost_estimate=pl.CostEstimate(flops=JOIN_COST, bytes_accessed=0, transcendentals=0),
        name="join_columns",
    )(*parts)


def middle_bits(n):
    bits, bit = [], 2
    while bit < n // 2:
        bits.append(bit)
        bit *= 2
    return bits


def gather_middle(values):
    parts = [values]
    for bit in middle_bits(lax.axis_size("tensor")):
        parts = parts + [swap(part, bit) for part in parts]
    return parts


def reduce_middle(parts):
    for bit in reversed(middle_bits(lax.axis_size("tensor"))):
        half = len(parts) // 2
        parts = [add_up(parts[i], swap(parts[half + i].astype(BF16), bit)) for i in range(half)]
    return parts[0]


def sum_of_products(left, right, start=None):
    total = dot(jnp.concatenate(left), jnp.concatenate(right), ((0,), (0,)))
    return total if start is None else start + total


def tie(*values):
    return lax.optimization_barrier(values)


def line_step(outer, own_in, sent_in, fresh, own_across, sent_across):
    rows, width = fresh.shape

    def kernel(outer_ref, a_ref, b_ref, c_ref, d_ref, e_ref, pair_ref, leaving_ref):
        @pl.when(outer_ref[0] == 1)
        def _():
            pair_ref[...] = c_ref[...]
            leaving_ref[...] = c_ref[...]

        @pl.when(outer_ref[0] == 0)
        def _():
            pair_ref[...] = (a_ref[...].astype(F32) + b_ref[...].astype(F32)).astype(BF16)
            leaving_ref[...] = (d_ref[...].astype(F32) + e_ref[...].astype(F32)).astype(BF16)

    steps = 4
    inner_block = pl.BlockSpec((rows, width // steps), lambda i, o: (0, i * (1 - o[0])))
    outer_block = pl.BlockSpec((rows, width // steps), lambda i, o: (0, i * o[0]))
    block = pl.BlockSpec((rows, width // steps), lambda i, o: (0, i))
    return pl.pallas_call(
        kernel,
        grid_spec=pltpu.PrefetchScalarGridSpec(
            num_scalar_prefetch=1,
            grid=(steps,),
            in_specs=[inner_block, inner_block, outer_block, inner_block, inner_block],
            out_specs=[block, block],
        ),
        out_shape=[jax.ShapeDtypeStruct((rows, width), BF16)] * 2,
        name="line_step",
    )(outer.astype(jnp.int32).reshape(1), own_in, sent_in, fresh, own_across, sent_across)


class LineSum:
    def __init__(self):
        self.line = lax.axis_size("dp") == 4
        place = lax.axis_index("dp")
        self.outer = (place == 0) | (place == 3)
        self.inward, self.across, self.outward = [], [], []
        self.sums = []

    def advance(self, arrays, others=()):
        if not self.line:
            self.sums += [lax.psum(a, "dp") for a in arrays]
            return others
        arrays, inward, across, outward, others = tie(
            list(arrays), self.inward, self.across, self.outward, others
        )
        self.inward, self.outward = [], []
        if len(arrays) == 1 and [a.shape for a, _ in inward + across] == [arrays[0].shape] * 2:
            pairs, leaving = line_step(self.outer, *inward[0], arrays[0], *across[0])
            sent = lax.ppermute(leaving, "dp", [(0, 1), (1, 0), (2, 3), (3, 2)])
            self.inward.append((arrays[0], sent))
            self.outward.append((leaving, sent))
            pairs = [pairs]
        else:
            pairs = [add_up(own, sent).astype(BF16) for own, sent in inward]
            totals = [add_up(own, sent).astype(BF16) for own, sent in across]
            self.inward = [(a, lax.ppermute(a, "dp", [(0, 1), (3, 2)])) for a in arrays]
            self.outward = [(a, lax.ppermute(a, "dp", [(1, 0), (2, 3)])) for a in totals]
        self.across = [(a, lax.ppermute(a, "dp", [(1, 2), (2, 1)])) for a in pairs]
        self.sums += [jnp.where(self.outer, sent, own) for own, sent in outward]
        return others


    def advance_and_peek(self):
        self.advance([])
        if not self.line:
            return self.sums[-2]
        own, sent = self.outward[-1]
        return jnp.where(self.outer, sent, own)


def tensor_bits():
    n, bits, bit = lax.axis_size("tensor"), [], 1
    while bit < n:
        bits.append(bit)
        bit *= 2
    return bits


def reduce_blocks(blocks):
    n, me = blocks.shape[0], lax.axis_index("tensor")
    held = [lax.dynamic_index_in_dim(blocks, me ^ r, 0, keepdims=False) for r in range(n)]
    for bit in tensor_bits():
        keep = jnp.stack([held[r] for r in range(len(held)) if r % 2 == 0])
        give = jnp.stack([held[r] for r in range(len(held)) if r % 2 == 1])
        total = add_up(keep, swap(give.astype(BF16), bit))
        held = [total[k] for k in range(total.shape[0])]
    return held[0]


def gather_blocks(block):
    n, me = lax.axis_size("tensor"), lax.axis_index("tensor")
    held = block[None]
    for bit in reversed(tensor_bits()):
        other = swap(held, bit)
        held = jnp.stack([held, other], 1).reshape(2 * held.shape[0], *block.shape)
    result = jnp.zeros_like(held)
    for r in range(n):
        result = lax.dynamic_update_index_in_dim(result, held[r], me ^ r, 0)
    return result


def gather_near(values):
    if lax.axis_size("tensor") != 8:
        return values, values
    return swap(values, 2), swap(values, 4)


def gather_pairs(values):
    parts, bits = [values], tensor_bits()
    for bit in bits:
        parts = parts + [swap(part, bit) for part in parts]
    return [(parts[i], parts[i + 1]) for i in range(0, len(parts), 2)]


def halves(value):
    rows = value.shape[0] // 2
    return value[:rows], value[rows:]


def reduce_begin(count, terms, between):
    n = lax.axis_size("tensor")
    if n != 8:
        parts = []
        for i in range(count):
            own, other = terms(i, None)
            parts.append(add_up(own, swap(other, 1)))
        while len(parts) > 1:
            half = len(parts) // 2
            parts = [add_up(parts[i], swap(parts[half + i].astype(BF16), 2 * half)) for i in range(half)]
        between(parts[0])
        return parts[0], ()
    own_d, other_d = (terms(3, None))
    core_d = swap(other_d, 1)
    own_y, other_y = (terms(2, own_d))
    core_y = swap(other_y, 1)
    diagonal = add_up(own_d, core_d).astype(BF16)
    diagonal, own_y = tie(diagonal, own_y)
    first, second = halves(diagonal)
    from_x, from_y = swap(first, 2), swap(second, 4)
    own_x, other_x = (terms(1, between(diagonal)))
    core_x = swap(other_x, 1)
    own, other = (terms(0, own_x))
    core = swap(other, 1)
    low, high = halves(add_up(own_y, core_y))
    for_y = jnp.concatenate([add_up(low, from_x), high]).astype(BF16)
    low, high = halves(add_up(own_x, core_x))
    for_x = jnp.concatenate([low, add_up(high, from_y)]).astype(BF16)
    return (own, core), (for_x, for_y)


def reduce_end(own, sent):
    if not sent:
        return own
    return add_up(*own, swap(sent[0], 2), swap(sent[1], 4))


def per_device(
    tokens,
    lengths,
    query_weight,
    key_weight,
    value_weight,
    output_weight,
    gate_weight,
    up_weight,
    down_weight,
    gain_attn,
    gain_mlp,
    pair_grad,
    cotangent,
):
    seqs, rows, width = tokens.shape
    n = lax.axis_size("tensor")
    me = lax.axis_index("tensor")
    top = n // 2
    flat = seqs * rows
    local_pos = me * rows + jnp.arange(rows)
    valid = (local_pos[None, :] < lengths[:, None]).astype(F32)[..., None]
    x = tokens.astype(F32)
    attn_gain = gain_attn.astype(F32)
    mlp_gain = gain_mlp.astype(F32)
    grad_y = cotangent.astype(F32)
    kv_weight = jnp.concatenate([key_weight, value_weight], axis=1)

    norm_in = normed(x, attn_gain).astype(BF16).reshape(flat, width)
    far_in = swap(norm_in, top)
    far_in = (far_in, swap(far_in, 1))
    near_in = (norm_in, swap(norm_in, 1))
    def slopes_of(blocks):
        return [dot(block, down_weight, ((1,), (1,))) for block in blocks]

    def with_core(part):
        return part, swap(part, 1)

    grad_out = (valid * grad_y).astype(BF16).reshape(flat, width)
    own_grads = with_core(grad_out)
    own_slopes, query_parts = tie(slopes_of(own_grads), gather_middle(query_weight))
    query_weights = join_columns(query_parts)
    heads_width = query_weights.shape[1]
    own_cos, own_sin = rope_block(me * rows, rows)
    kv_raw = dot(norm_in, kv_weight, ((1,), (0,))).reshape(seqs, rows, 2 * HEAD)
    key_raw = kv_raw[..., :HEAD]
    key_own = key_raw * own_cos + jnp.roll(key_raw, HEAD // 2, axis=-1) * own_sin
    kv_own = jnp.concatenate([key_own, kv_raw[..., HEAD:]], axis=-1).astype(BF16)

    output_weight, kv_own = tie(output_weight, kv_own)
    output_parts = gather_middle(output_weight)
    kv = lax.all_gather(kv_own, "tensor", axis=1, tiled=True)

    def place_of(offset):
        place = jnp.stack([me ^ offset, me ^ (offset + 1)]).astype(jnp.int32)
        blocks = [rope_block(place[i] * rows, rows) for i in range(2)]
        return place, (jnp.stack([b[0] for b in blocks]), jnp.stack([b[1] for b in blocks]))

    def attend(part, place, table):
        return attention_forward(place, lengths, part, query_weights, kv, *table)

    def portions_of(mixed):
        return [dot(mixed[i], output_weights, ((1,), (0,)), BF16) for i in range(2)]

    near_place, near_table = place_of(0)
    far_place, far_table = place_of(top)
    grad_out, _ = tie(grad_out, norm_in)
    grad_far = swap(grad_out, top)
    near_result = attend(near_in, near_place, near_table)
    far_in, _ = tie(far_in, near_result[0])
    far_result = attend(far_in, far_place, far_table)
    output_parts, far_mixed, grad_far = tie(output_parts, far_result[0], grad_far)
    output_weights = jnp.concatenate(output_parts, axis=0)
    far_portions = portions_of(far_mixed)
    for_far = add_up(far_portions[0], swap(far_portions[1], 1)).astype(BF16)
    for_far, near_mixed = tie(for_far, near_result[0])
    from_far = swap(for_far, top)
    near_portions = portions_of(near_mixed)
    near_core = swap(near_portions[1], 1)
    if n == 8:
        grad_out, _ = tie(grad_out, far_mixed)
        grad_side = swap(grad_out, 2)
        size = flat // 2
        from_far, grad_side, grad_far = tie(from_far, grad_side, grad_far)
        grad_diagonal = [swap(grad_side[:size], 4), swap(grad_far[size:], 2)]
    attn_out = add_up(near_portions[0], near_core, from_far)
    hidden = x + valid * attn_out.reshape(seqs, rows, width)

    chips = n // 2
    norm_mid = normed(hidden, mlp_gain).astype(BF16).reshape(flat, width)
    gate_rows, up_rows = gate_weight.T, up_weight.T

    mids, acts, g_gates, g_ups = [], [], [], []

    def forward_blocks(blocks, slopes):
        for mid, slope in zip(blocks, slopes):
            gate = dot(mid, gate_rows, ((1,), (1,)))
            up = dot(mid, up_rows, ((1,), (1,)))
            sig = 1.0 / (1.0 + jnp.exp(-gate))
            silu = gate * sig
            mids.append(mid)
            acts.append((silu * up).astype(BF16))
            g_gates.append((slope * up * sig * (1.0 + gate * (1.0 - sig))).astype(BF16))
            g_ups.append((slope * silu).astype(BF16))

    def diagonal_blocks(parts):
        return [jnp.concatenate(p) for p in zip(*[with_core(part) for part in parts])]

    if n == 8:
        at_x, at_y = gather_near(norm_mid)
        grads = [*own_grads, *with_core(grad_side), *with_core(grad_far)]
        slopes = own_slopes + slopes_of(grads[2:])
        forward_blocks(with_core(norm_mid), slopes[:2])
        at_x, at_y, slopes, acts[1] = tie(at_x, at_y, slopes, acts[1])
        diagonal = [swap(at_x[:size], 4), swap(at_y[size:], 2)]
        forward_blocks((*with_core(at_x), *with_core(at_y)), slopes[2:6])
        grad_down = sum_of_products(acts[:6], grads[:6])
        diagonal, grad_diagonal, grad_down = tie(diagonal, grad_diagonal, grad_down)
        grads += diagonal_blocks(grad_diagonal)
        forward_blocks(diagonal_blocks(diagonal), slopes_of(grads[6:]))
    else:
        grads = [block for pair in gather_pairs(grad_out) for block in pair]
        forward_blocks([block for pair in gather_pairs(norm_mid) for block in pair], slopes_of(grads))
        grad_down = sum_of_products(acts[:-2], grads[:-2])

    def mid_term(r):
        terms = dot(g_gates[r], gate_rows, ((1,), (0,))) + dot(g_ups[r], up_rows, ((1,), (0,)))
        return terms.astype(BF16)

    def mid_terms(i, after):
        for k in (2 * i, 2 * i + 1):
            if after is not None:
                g_gates[k], g_ups[k], _ = tie(g_gates[k], g_ups[k], after)
        return mid_term(2 * i), mid_term(2 * i + 1)

    sums, down_parts = LineSum(), []

    def down_gradient(after):
        last, after = tie(acts[-2:], after)
        down_parts.extend(halves(sum_of_products(last, grads[-2:], grad_down).astype(BF16)))
        return sums.advance([down_parts[0]], after)

    mid_own, mid_sent = reduce_begin(chips, mid_terms, down_gradient)
    grad_mid = reduce_end(mid_own, mid_sent).reshape(seqs, rows, width)

    g_gates, g_ups, mids = sums.advance([down_parts[1]], (g_gates, g_ups, mids))
    mid_all = [jnp.concatenate(mids)]
    grad_gate = halves(sum_of_products(g_gates, mid_all).astype(BF16))
    back, mlp_gain_part = norm_back(hidden, mlp_gain, grad_mid)
    grad_hidden = grad_y + back
    grad_attn = (valid * grad_hidden).astype(BF16).reshape(flat, width)
    far_grad = swap(grad_attn, top)
    near_grad = (grad_attn, swap(grad_attn, 1))

    def attend_back(part, result, place, table):
        return attention_backward(
            place, lengths, part, output_weights, query_weights, result[1], result[2], kv, *table
        )

    def product(left, right):
        return dot(jnp.concatenate(left), jnp.concatenate(right), ((0,), (0,)), BF16)

    g_ups, near_grad = sums.advance([grad_gate[0]], (g_ups, near_grad))
    grad_up = halves(sum_of_products(g_ups, mid_all).astype(BF16))
    near_q, near_terms, near_kv = attend_back(near_grad, near_result, near_place, near_table)
    near_core = swap(near_terms[1], 1)

    far_grad, near_q, near_kv = sums.advance([grad_gate[1]], (far_grad, near_q, near_kv))
    far_grad = (far_grad, swap(far_grad, 1))
    far_q, far_terms, far_kv = attend_back(far_grad, far_result, far_place, far_table)
    for_far = add_up(far_terms[0], swap(far_terms[1], 1)).astype(BF16)
    from_far = swap(for_far, top)

    far_grad, far_q, far_kv = sums.advance([grad_up[0]], (far_grad, far_q, far_kv))
    unit = output_weight.shape[0]
    kv_blocks = (near_kv + far_kv).astype(BF16).reshape(seqs, n, rows, 2 * HEAD).swapaxes(0, 1)
    kv_sum = reduce_blocks(kv_blocks)
    mixed = [r[0][i] for r in (near_result, far_result) for i in range(2)]
    wo_full = product(mixed, [*near_grad, *far_grad])
    wo_full, kv_sum = tie(wo_full, kv_sum)
    wo_part = reduce_middle([wo_full[i * unit : (i + 1) * unit] for i in range(heads_width // unit)])
    wo_part = wo_part.astype(BF16)
    key_grad = kv_sum[..., :HEAD]
    key_grad = key_grad * own_cos - jnp.roll(key_grad, HEAD // 2, axis=-1) * own_sin
    kv_grad = jnp.concatenate([key_grad, kv_sum[..., HEAD:]], -1).astype(BF16).reshape(flat, 2 * HEAD)

    from_far, far_q, kv_grad = sums.advance([grad_up[1]], (from_far, far_q, kv_grad))
    grad_in = add_up(near_terms[0], near_core, from_far)
    grad_in = grad_in + dot(kv_grad, kv_weight, ((1,), (1,)))
    kv_portion = dot(norm_in, kv_grad, ((0,), (0,)))
    back, attn_gain_part = norm_back(x, attn_gain, grad_in.reshape(seqs, rows, width))
    grad_tokens = grad_hidden + back
    gains = jnp.concatenate([attn_gain_part, mlp_gain_part]).reshape(-1, 2 * HEAD)
    shared = jnp.concatenate([kv_portion + pair_grad[0, 0], gains])
    shared = jnp.pad(shared, ((0, -shared.shape[0] % (16 * n)), (0, 0))).astype(BF16)
    shared = reduce_blocks(shared.reshape(n, -1, 2 * HEAD)).astype(BF16)


    wq_full = product([near_q[0], near_q[1], far_q[0], far_q[1]], [*near_in, *far_in])
    wq_full, shared = tie(wq_full, shared)
    wq_part = reduce_middle([wq_full[i * unit : (i + 1) * unit] for i in range(heads_width // unit)])
    wq_part = wq_part.astype(BF16)

    acts = sums.advance([wo_part, shared], acts)

    def out_terms(i, after):
        left = acts[2 * i : 2 * i + 2]
        left = left if after is None else tie(left, after)[0]
        return [dot(part, down_weight, ((1,), (0,)), BF16) for part in left]

    out_own, out_sent = reduce_begin(chips, out_terms, lambda after: after)
    rows_out = reduce_end(out_own, out_sent)
    output = (hidden + valid * rows_out.reshape(seqs, rows, width)).astype(BF16)
    sums.advance([wq_part])
    shared = sums.advance_and_peek()
    shared = sums.advance([], gather_blocks(shared))
    sums.advance([])
    down_1, down_2, gate_1, gate_2, up_1, up_2, wo_sum, _, wq_sum = sums.sums
    shared = shared.reshape(-1, 2 * HEAD).astype(F32)
    gains = shared[width : width + gains.shape[0]].reshape(2, width)
    return (
        output,
        grad_tokens,
        wq_sum.astype(F32).T,
        shared[:width, :HEAD],
        shared[:width, HEAD:],
        wo_sum.astype(F32),
        jnp.concatenate([gate_1, gate_2]).astype(F32).T,
        jnp.concatenate([up_1, up_2]).astype(F32).T,
        jnp.concatenate([down_1, down_2]).astype(F32),
        gains[0],
        gains[1],
    )


def solution(mesh):
    placed = (
        P("dp", "tensor", None),
        P("dp"),
        P(None, "tensor"),
        P(),
        P(),
        P("tensor", None),
        P(None, "tensor"),
        P(None, "tensor"),
        P("tensor", None),
        P(),
        P(),
        P("dp", "tensor", None, None),
        P("dp", "tensor", None),
    )
    return jax.shard_map(
        per_device,
        mesh=mesh,
        in_specs=placed,
        out_specs=(
            P("dp", "tensor", None),
            P("dp", "tensor", None),
            P(None, "tensor"),
            P(),
            P(),
            P("tensor", None),
            P(None, "tensor"),
            P(None, "tensor"),
            P("tensor", None),
            P(),
            P(),
        ),
        check_vma=False,
    )
```

profile of v0, /device:TPU:0, one launch (start us, length us, event | category | flops | bytes accessed | tf_op | source)
XLA Modules:
  0.0 586.1 jit_solution(4971170592824224856)
XLA Ops:
  37.0 18.8 %collective-permute-done.5.refs_1_ = bf16[2048,256]{1,0:T(8,128)(2,1)S(1)} collective-permute-done((bf16[2048,256]{1,0:T(8,128)(2,1)}, bf16[2048,256]{1,0:T(8,128)(2,1)S(1)}, u32[]{:S(2)}, u32[]{:S(2)}) %collective-permute-start.5) | collective-permute-done | bytes 1048608 | tf_op jit(solution)/shard_map/ppermute | solution.py:50
  63.6 7.5 %attention_forward.2 = (bf16[2,256,512]{2,1,0:T(8,128)(2,1)S(1)}, bf16[2,2,512,128]{3,2,1,0:T(8,128)(2,1)S(1)}, f32[2,2,8,512]{3,2,1,0:T(8,128)S(1)}) custom-call(s32[2]{0:T(128)S(1)} %pad_add_fusion.1.place, s32[2]{0:T(128)S(1)} %copy-done.14, bf16[256,2048]{1,0:T(8,128)(2,1)} %bitcast.3.x0_ref, bf16[256,2048]{1,0:T(8,128)(2,1)} %collective-permute-done.3.x1_ref, ...), custom_call_target="tpu_custom_call" | custom-call | flops 8053063680 | bytes 524288 | tf_op jit(solution)/shard_map/attention_forward/pallas_call | solution.py:156
  72.6 9.3 %attention_forward.3 = (bf16[2,256,512]{2,1,0:T(8,128)(2,1)S(1)}, bf16[2,2,512,128]{3,2,1,0:T(8,128)(2,1)S(1)}, f32[2,2,8,512]{3,2,1,0:T(8,128)S(1)}) custom-call(s32[2]{0:T(128)S(1)} %pad_add_fusion.place, s32[2]{0:T(128)S(1)} %copy-done.14, bf16[256,2048]{1,0:T(8,128)(2,1)} %collective-permute-done.1.x0_ref, ...), custom_call_target="tpu_custom_call" | custom-call | flops 8053063680 | bytes 524288 | tf_op jit(solution)/shard_map/attention_forward/pallas_call | solution.py:156
  95.4 16.3 %collective-permute-done.10 = bf16[256,2048]{1,0:T(8,128)(2,1)} collective-permute-done((bf16[256,2048]{1,0:T(8,128)(2,1)}, bf16[256,2048]{1,0:T(8,128)(2,1)}, u32[]{:S(2)}, u32[]{:S(2)}) %collective-permute-start.10) | collective-permute-done | bytes 1048608 | tf_op jit(solution)/shard_map/ppermute | solution.py:50
  162.3 4.7 fusion.160
  217.3 15.5 %collective-permute-done.27 = bf16[352,2048]{1,0:T(8,128)(2,1)S(1)} collective-permute-done((bf16[352,2048]{1,0:T(8,128)(2,1)S(1)}, bf16[352,2048]{1,0:T(8,128)(2,1)S(1)}, u32[]{:S(2)}, u32[]{:S(2)}) %collective-permute-start.27) | collective-permute-done | bytes 1441824 | tf_op jit(solution)/shard_map/ppermute | solution.py:366
  236.4 7.1 %collective-permute-start.28 = (bf16[352,2048]{1,0:T(8,128)(2,1)}, bf16[352,2048]{1,0:T(8,128)(2,1)}, u32[]{:S(2)}, u32[]{:S(2)}) collective-permute-start(bf16[352,2048]{1,0:T(8,128)(2,1)} %get-tuple-element.296.a_ref), channel_id=1, source_target_pairs={{0,8},{24,16},{1,9},{25,17},{2,10},{26,18},{3,11},{27,19},{4,12},{... | collective-permute-start | bytes 4325384 | tf_op jit(solution)/shard_map/ppermute | solution.py:366
  252.0 6.4 %convolution_convert_fusion.1 = bf16[704,2048]{1,0:T(8,128)(2,1)S(1)} fusion(bf16[2048,704]{0,1:T(8,128)(2,1)S(1)} %constant_dynamic-update-slice_fusion.20, bf16[2048,2048]{1,0:T(8,128)(2,1)S(1)} %constant_dynamic-update-slice_fusion.28), kind=kOutput, calls=%fused_computation.26 | convolution fusion | flops 5907021824 | bytes 14155776 | tf_op jit(solution)/shard_map/dot_general | solution.py:54
  261.7 11.1 %collective-permute-done.28.b_ref = bf16[352,2048]{1,0:T(8,128)(2,1)} collective-permute-done((bf16[352,2048]{1,0:T(8,128)(2,1)}, bf16[352,2048]{1,0:T(8,128)(2,1)}, u32[]{:S(2)}, u32[]{:S(2)}) %collective-permute-start.28) | collective-permute-done | bytes 1441824 | tf_op jit(solution)/shard_map/ppermute | solution.py:366
  284.2 8.5 %convolution_convert_fusion = bf16[704,2048]{1,0:T(8,128)(2,1)S(1)} fusion(bf16[2048,704]{0,1:T(8,128)(2,1)S(1)} %constant_dynamic-update-slice_fusion.36, bf16[2048,2048]{1,0:T(8,128)(2,1)} %copy-done.115), kind=kOutput, calls=%fused_computation.25 | convolution fusion | flops 5907021824 | bytes 14155776 | tf_op jit(solution)/shard_map/dot_general | solution.py:54
  292.7 13.0 %attention_backward.2 = (bf16[2,256,512]{2,1,0:T(8,128)(2,1)}, bf16[2,256,2048]{2,1,0:T(8,128)(2,1)}, f32[2,1024,256]{2,1,0:T(8,128)}) custom-call(s32[2]{0:T(128)} %copy-done.16, s32[2]{0:T(128)} %lengths.7, bf16[256,2048]{1,0:T(8,128)(2,1)} %bitcast.26.g0_ref, bf16[256,2048]{1,0:T(8,128)(2,1)} %collective-permute-done.37.g1_ref, ...), custom_call_target="tpu_custom_call" | custom-call | flops 134217728 | bytes 524288 | tf_op jit(solution)/shard_map/attention_backward/pallas_call | solution.py:241
  327.3 15.8 %attention_backward.3 = (bf16[2,256,512]{2,1,0:T(8,128)(2,1)}, bf16[2,256,2048]{2,1,0:T(8,128)(2,1)}, f32[2,1024,256]{2,1,0:T(8,128)}) custom-call(s32[2]{0:T(128)} %copy-done.15, s32[2]{0:T(128)} %lengths.7, bf16[256,2048]{1,0:T(8,128)(2,1)} %collective-permute-done.40.g0_ref, bf16[256,2048]{1,0:T(8,128)(2,1)} %collective-permute-done.43.g1_ref, ...), custom_call_target="tpu_custom_call" | custom-call | flops 134217728 | bytes 524288 | tf_op jit(solution)/shard_map/attention_backward/pallas_call | solution.py:241
  345.9 6.6 %collective-permute-done.41.b_ref = bf16[352,2048]{1,0:T(8,128)(2,1)S(1)} collective-permute-done((bf16[352,2048]{1,0:T(8,128)(2,1)}, bf16[352,2048]{1,0:T(8,128)(2,1)S(1)}, u32[]{:S(2)}, u32[]{:S(2)}) %collective-permute-start.41) | collective-permute-done | bytes 1441824 | tf_op jit(solution)/shard_map/ppermute | solution.py:359
  366.7 5.0 fusion.19
  385.7 18.4 %collective-permute-done.46 = bf16[1,2,128,256]{3,2,1,0:T(8,128)(2,1)S(1)} collective-permute-done((bf16[1,2,128,256]{3,2,1,0:T(8,128)(2,1)S(1)}, bf16[1,2,128,256]{3,2,1,0:T(8,128)(2,1)S(1)}, u32[]{:S(2)}, u32[]{:S(2)}) %collective-permute-start.46) | collective-permute-done | bytes 131104 | tf_op jit(solution)/shard_map/ppermute | solution.py:50
  422.8 4.7 fusion.16
  430.1 7.5 %collective-permute-done.54 = bf16[2,272,256]{2,1,0:T(8,128)(2,1)S(1)} collective-permute-done((bf16[2,272,256]{2,1,0:T(8,128)(2,1)S(1)}, bf16[2,272,256]{2,1,0:T(8,128)(2,1)S(1)}, u32[]{:S(2)}, u32[]{:S(2)}) %collective-permute-start.54) | collective-permute-done | bytes 278560 | tf_op jit(solution)/shard_map/ppermute | solution.py:50
  450.6 8.1 %collective-permute-start.67 = (bf16[256,2048]{1,0:T(8,128)(2,1)S(1)}, bf16[256,2048]{1,0:T(8,128)(2,1)S(1)}, u32[]{:S(2)}, u32[]{:S(2)}) collective-permute-start(bf16[256,2048]{1,0:T(8,128)(2,1)S(1)} %add_convert_fusion.12), channel_id=1, source_target_pairs={{0,8},{24,16},{1,9},{25,17},{2,10},{26,18},{3,11},{27,19},{4,12},{... | collective-permute-start | bytes 3145736 | tf_op jit(solution)/shard_map/ppermute | solution.py:366
  473.1 8.4 %collective-permute-done.68 = bf16[272,256]{1,0:T(8,128)(2,1)S(1)} collective-permute-done((bf16[272,256]{1,0:T(8,128)(2,1)S(1)}, bf16[272,256]{1,0:T(8,128)(2,1)S(1)}, u32[]{:S(2)}, u32[]{:S(2)}) %collective-permute-start.68) | collective-permute-done | bytes 139296 | tf_op jit(solution)/shard_map/ppermute | solution.py:366
  486.5 6.1 %collective-permute-done.64 = bf16[128,2048]{1,0:T(8,128)(2,1)S(1)} collective-permute-done((bf16[128,2048]{1,0:T(8,128)(2,1)S(1)}, bf16[128,2048]{1,0:T(8,128)(2,1)S(1)}, u32[]{:S(2)}, u32[]{:S(2)}) %collective-permute-start.64) | collective-permute-done | bytes 524320 | tf_op jit(solution)/shard_map/ppermute | solution.py:50
  493.6 7.4 %collective-permute-start.71 = (bf16[256,2048]{1,0:T(8,128)(2,1)S(1)}, bf16[256,2048]{1,0:T(8,128)(2,1)S(1)}, u32[]{:S(2)}, u32[]{:S(2)}) collective-permute-start(bf16[256,2048]{1,0:T(8,128)(2,1)S(1)} %add_convert_fusion.9), channel_id=1, source_target_pairs={{0,8},{24,16},{1,9},{25,17},{2,10},{26,18},{3,11},{27,19},{4,12},{... | collective-permute-start | bytes 3145736 | tf_op jit(solution)/shard_map/ppermute | solution.py:366
  506.1 12.9 %collective-permute-done.71 = bf16[256,2048]{1,0:T(8,128)(2,1)S(1)} collective-permute-done((bf16[256,2048]{1,0:T(8,128)(2,1)S(1)}, bf16[256,2048]{1,0:T(8,128)(2,1)S(1)}, u32[]{:S(2)}, u32[]{:S(2)}) %collective-permute-start.71) | collective-permute-done | bytes 1048608 | tf_op jit(solution)/shard_map/ppermute | solution.py:366
  534.5 5.6 collective-permute-done.79
  550.9 23.4 %collective-permute-done.81 = bf16[256,2048]{1,0:T(8,128)(2,1)S(1)} collective-permute-done((bf16[256,2048]{1,0:T(8,128)(2,1)S(1)}, bf16[256,2048]{1,0:T(8,128)(2,1)S(1)}, u32[]{:S(2)}, u32[]{:S(2)}) %collective-permute-start.81) | collective-permute-done | bytes 1048608 | tf_op jit(solution)/shard_map/ppermute | solution.py:367
  (679 shorter events, 320.3 us)
Async XLA Ops:
  7.2 53.4 %all-gather.2.cloned.1.call-start = ((), (), s32[]{:S(2)}) async-start(), calls=%async_computation | async-start | bytes 1179648 | tf_op jit(solution)/shard_map/all_gather | solution.py:518
  12.7 47.9 %collective-permute-start.3 = (bf16[256,2048]{1,0:T(8,128)(2,1)}, bf16[256,2048]{1,0:T(8,128)(2,1)}, u32[]{:S(2)}, u32[]{:S(2)}) collective-permute-start(bf16[256,2048]{1,0:T(8,128)(2,1)} %bitcast.3.x0_ref), channel_id=1, source_target_pairs={{0,1},{1,0},{2,3},{3,2},{4,5},{5,4},{6,7},{7,6},{8,9},{9,8},{10,11... | collective-permute-start | bytes 3145736 | tf_op jit(solution)/shard_map/ppermute | solution.py:50
  13.1 43.7 %collective-permute-start.1 = (bf16[256,2048]{1,0:T(8,128)(2,1)}, bf16[256,2048]{1,0:T(8,128)(2,1)}, u32[]{:S(2)}, u32[]{:S(2)}) collective-permute-start(bf16[256,2048]{1,0:T(8,128)(2,1)} %bitcast.3.x0_ref), channel_id=1, source_target_pairs={{0,4},{1,5},{2,6},{3,7},{4,0},{5,1},{6,2},{7,3},{8,12},{9,13},{10,... | collective-permute-start | bytes 3145736 | tf_op jit(solution)/shard_map/ppermute | solution.py:50
  26.9 55.1 %collective-permute-start = (bf16[256,2048]{1,0:T(8,128)(2,1)}, bf16[256,2048]{1,0:T(8,128)(2,1)}, u32[]{:S(2)}, u32[]{:S(2)}) collective-permute-start(bf16[256,2048]{1,0:T(8,128)(2,1)} %param.18), channel_id=1, source_target_pairs={{0,2},{1,3},{2,0},{3,1},{4,6},{5,7},{6,4},{7,5},{8,10},{9,11},{10,... | collective-permute-start | bytes 3145736 | tf_op jit(solution)/shard_map/ppermute | solution.py:50
  34.9 47.1 %collective-permute-start.6 = (bf16[256,2048]{1,0:T(8,128)(2,1)}, bf16[256,2048]{1,0:T(8,128)(2,1)}, u32[]{:S(2)}, u32[]{:S(2)}) collective-permute-start(bf16[256,2048]{1,0:T(8,128)(2,1)} %bitcast.6), channel_id=1, source_target_pairs={{0,4},{1,5},{2,6},{3,7},{4,0},{5,1},{6,2},{7,3},{8,12},{9,13},{10,... | collective-permute-start | bytes 3145736 | tf_op jit(solution)/shard_map/ppermute | solution.py:50
  134.0 33.1 %collective-permute-start.18 = (bf16[128,2048]{1,0:T(8,128)(2,1)S(1)}, bf16[128,2048]{1,0:T(8,128)(2,1)S(1)}, u32[]{:S(2)}, u32[]{:S(2)}) collective-permute-start(bf16[128,2048]{1,0:T(8,128)(2,1)S(1)} %slice.259), channel_id=1, source_target_pairs={{0,4},{1,5},{2,6},{3,7},{4,0},{5,1},{6,2},{7,3},{8,12},{9,13},{10,... | collective-permute-start | bytes 1572872 | tf_op jit(solution)/shard_map/ppermute | solution.py:50
  200.0 32.7 %collective-permute-start.27 = (bf16[352,2048]{1,0:T(8,128)(2,1)S(1)}, bf16[352,2048]{1,0:T(8,128)(2,1)S(1)}, u32[]{:S(2)}, u32[]{:S(2)}) collective-permute-start(bf16[352,2048]{1,0:T(8,128)(2,1)S(1)} %get-tuple-element.274), channel_id=1, source_target_pairs={{0,8},{24,16},{1,9},{25,17},{2,10},{26,18},{3,11},{27,19},{4,12},{... | collective-permute-start | bytes 4325384 | tf_op jit(solution)/shard_map/ppermute | solution.py:366
  205.7 41.8 %collective-permute-start.30 = (bf16[256,2048]{1,0:T(8,128)(2,1)S(1)}, bf16[256,2048]{1,0:T(8,128)(2,1)S(1)}, u32[]{:S(2)}, u32[]{:S(2)}) collective-permute-start(bf16[256,2048]{1,0:T(8,128)(2,1)S(1)} %fusion.27), channel_id=1, source_target_pairs={{0,1},{1,0},{2,3},{3,2},{4,5},{5,4},{6,7},{7,6},{8,9},{9,8},{10,11... | collective-permute-start | bytes 3145736 | tf_op jit(solution)/shard_map/ppermute | solution.py:50
  210.1 37.5 %collective-permute-start.33 = (bf16[256,2048]{1,0:T(8,128)(2,1)S(1)}, bf16[256,2048]{1,0:T(8,128)(2,1)S(1)}, u32[]{:S(2)}, u32[]{:S(2)}) collective-permute-start(bf16[256,2048]{1,0:T(8,128)(2,1)S(1)} %pad_maximum_fusion.1), channel_id=1, source_target_pairs={{0,2},{1,3},{2,0},{3,1},{4,6},{5,7},{6,4},{7,5},{8,10},{9,11},{10,... | collective-permute-start | bytes 3145736 | tf_op jit(solution)/shard_map/ppermute | solution.py:50
  214.4 33.2 %collective-permute-start.36 = (bf16[256,2048]{1,0:T(8,128)(2,1)S(1)}, bf16[256,2048]{1,0:T(8,128)(2,1)S(1)}, u32[]{:S(2)}, u32[]{:S(2)}) collective-permute-start(bf16[256,2048]{1,0:T(8,128)(2,1)S(1)} %pad_maximum_fusion.2), channel_id=1, source_target_pairs={{0,4},{1,5},{2,6},{3,7},{4,0},{5,1},{6,2},{7,3},{8,12},{9,13},{10,... | collective-permute-start | bytes 3145736 | tf_op jit(solution)/shard_map/ppermute | solution.py:50
  236.4 36.4 %collective-permute-start.28 = (bf16[352,2048]{1,0:T(8,128)(2,1)}, bf16[352,2048]{1,0:T(8,128)(2,1)}, u32[]{:S(2)}, u32[]{:S(2)}) collective-permute-start(bf16[352,2048]{1,0:T(8,128)(2,1)} %get-tuple-element.296.a_ref), channel_id=1, source_target_pairs={{0,8},{24,16},{1,9},{25,17},{2,10},{26,18},{3,11},{27,19},{4,12},{... | collective-permute-start | bytes 4325384 | tf_op jit(solution)/shard_map/ppermute | solution.py:366
  260.4 47.4 %collective-permute-start.40 = (bf16[256,2048]{1,0:T(8,128)(2,1)}, bf16[256,2048]{1,0:T(8,128)(2,1)}, u32[]{:S(2)}, u32[]{:S(2)}) collective-permute-start(bf16[256,2048]{1,0:T(8,128)(2,1)} %bitcast.26.g0_ref), channel_id=1, source_target_pairs={{0,4},{1,5},{2,6},{3,7},{4,0},{5,1},{6,2},{7,3},{8,12},{9,13},{10,... | collective-permute-start | bytes 3145736 | tf_op jit(solution)/shard_map/ppermute | solution.py:50
  277.4 33.7 %collective-permute-start.38 = (bf16[352,2048]{1,0:T(8,128)(2,1)}, bf16[352,2048]{1,0:T(8,128)(2,1)}, u32[]{:S(2)}, u32[]{:S(2)}) collective-permute-start(bf16[352,2048]{1,0:T(8,128)(2,1)} %get-tuple-element.398), channel_id=1, source_target_pairs={{0,8},{8,0},{16,24},{24,16},{1,9},{9,1},{17,25},{25,17},{2,10},{10... | collective-permute-start | bytes 4325384 | tf_op jit(solution)/shard_map/ppermute | solution.py:359
  315.5 37.0 %collective-permute-start.41 = (bf16[352,2048]{1,0:T(8,128)(2,1)}, bf16[352,2048]{1,0:T(8,128)(2,1)S(1)}, u32[]{:S(2)}, u32[]{:S(2)}) collective-permute-start(bf16[352,2048]{1,0:T(8,128)(2,1)} %get-tuple-element.400), channel_id=1, source_target_pairs={{0,8},{8,0},{16,24},{24,16},{1,9},{9,1},{17,25},{25,17},{2,10},{10... | collective-permute-start | bytes 4325384 | tf_op jit(solution)/shard_map/ppermute | solution.py:359
  320.0 32.4 %collective-permute-start.42 = (bf16[352,2048]{1,0:T(8,128)(2,1)}, bf16[352,2048]{1,0:T(8,128)(2,1)S(1)}, u32[]{:S(2)}, u32[]{:S(2)}) collective-permute-start(bf16[352,2048]{1,0:T(8,128)(2,1)} %get-tuple-element.327.d_ref), channel_id=1, source_target_pairs={{8,16},{16,8},{9,17},{17,9},{10,18},{18,10},{11,19},{19,11},{12,20... | collective-permute-start | bytes 4325384 | tf_op jit(solution)/shard_map/ppermute | solution.py:368
  323.6 91.4 %collective-permute-start.52 = (bf16[256,2048]{1,0:T(8,128)(2,1)}, bf16[256,2048]{1,0:T(8,128)(2,1)}, u32[]{:S(2)}, u32[]{:S(2)}) collective-permute-start(bf16[256,2048]{1,0:T(8,128)(2,1)} %slice_bitcast_fusion), channel_id=1, source_target_pairs={{0,1},{1,0},{2,3},{3,2},{4,5},{5,4},{6,7},{7,6},{8,9},{9,8},{10,11... | collective-permute-start | bytes 3145736 | tf_op jit(solution)/shard_map/ppermute | solution.py:50
  360.8 45.5 %collective-permute-start.48 = (bf16[352,2048]{1,0:T(8,128)(2,1)}, bf16[352,2048]{1,0:T(8,128)(2,1)}, u32[]{:S(2)}, u32[]{:S(2)}) collective-permute-start(bf16[352,2048]{1,0:T(8,128)(2,1)} %get-tuple-element.390), channel_id=1, source_target_pairs={{0,8},{8,0},{16,24},{24,16},{1,9},{9,1},{17,25},{25,17},{2,10},{10... | collective-permute-start | bytes 4325384 | tf_op jit(solution)/shard_map/ppermute | solution.py:359
  364.7 41.6 %collective-permute-start.49 = (bf16[352,2048]{1,0:T(8,128)(2,1)}, bf16[352,2048]{1,0:T(8,128)(2,1)}, u32[]{:S(2)}, u32[]{:S(2)}) collective-permute-start(bf16[352,2048]{1,0:T(8,128)(2,1)} %get-tuple-element.342.d_ref), channel_id=1, source_target_pairs={{8,16},{16,8},{9,17},{17,9},{10,18},{18,10},{11,19},{19,11},{12,20... | collective-permute-start | bytes 4325384 | tf_op jit(solution)/shard_map/ppermute | solution.py:368
  405.2 33.2 %collective-permute-start.47 = (bf16[256,2048]{1,0:T(8,128)(2,1)}, bf16[256,2048]{1,0:T(8,128)(2,1)}, u32[]{:S(2)}, u32[]{:S(2)}) collective-permute-start(bf16[256,2048]{1,0:T(8,128)(2,1)} %slice.279), channel_id=1, source_target_pairs={{0,2},{1,3},{2,0},{3,1},{4,6},{5,7},{6,4},{7,5},{8,10},{9,11},{10,... | collective-permute-start | bytes 3145736 | tf_op jit(solution)/shard_map/ppermute | solution.py:50
  410.7 33.5 %collective-permute-start.56 = (bf16[352,2048]{1,0:T(8,128)(2,1)}, bf16[352,2048]{1,0:T(8,128)(2,1)}, u32[]{:S(2)}, u32[]{:S(2)}) collective-permute-start(bf16[352,2048]{1,0:T(8,128)(2,1)} %get-tuple-element.392), channel_id=1, source_target_pairs={{0,8},{8,0},{16,24},{24,16},{1,9},{9,1},{17,25},{25,17},{2,10},{10... | collective-permute-start | bytes 4325384 | tf_op jit(solution)/shard_map/ppermute | solution.py:359
  446.2 37.2 %collective-permute-start.70 = (bf16[352,2048]{1,0:T(8,128)(2,1)S(1)}, bf16[352,2048]{1,0:T(8,128)(2,1)S(1)}, u32[]{:S(2)}, u32[]{:S(2)}) collective-permute-start(bf16[352,2048]{1,0:T(8,128)(2,1)S(1)} %add_convert_fusion.2), channel_id=1, source_target_pairs={{8,0},{16,24},{9,1},{17,25},{10,2},{18,26},{11,3},{19,27},{12,4},{... | collective-permute-start | bytes 4325384 | tf_op jit(solution)/shard_map/ppermute | solution.py:367
  449.7 33.7 %collective-permute-start.69 = (bf16[352,2048]{1,0:T(8,128)(2,1)S(1)}, bf16[352,2048]{1,0:T(8,128)(2,1)S(1)}, u32[]{:S(2)}, u32[]{:S(2)}) collective-permute-start(bf16[352,2048]{1,0:T(8,128)(2,1)S(1)} %add_convert_fusion.3), channel_id=1, source_target_pairs={{8,16},{16,8},{9,17},{17,9},{10,18},{18,10},{11,19},{19,11},{12,20... | collective-permute-start | bytes 4325384 | tf_op jit(solution)/shard_map/ppermute | solution.py:368
  450.6 31.8 %collective-permute-start.67 = (bf16[256,2048]{1,0:T(8,128)(2,1)S(1)}, bf16[256,2048]{1,0:T(8,128)(2,1)S(1)}, u32[]{:S(2)}, u32[]{:S(2)}) collective-permute-start(bf16[256,2048]{1,0:T(8,128)(2,1)S(1)} %add_convert_fusion.12), channel_id=1, source_target_pairs={{0,8},{24,16},{1,9},{25,17},{2,10},{26,18},{3,11},{27,19},{4,12},{... | collective-permute-start | bytes 3145736 | tf_op jit(solution)/shard_map/ppermute | solution.py:366
  483.9 35.1 %collective-permute-start.74 = (bf16[352,2048]{1,0:T(8,128)(2,1)S(1)}, bf16[352,2048]{1,0:T(8,128)(2,1)S(1)}, u32[]{:S(2)}, u32[]{:S(2)}) collective-permute-start(bf16[352,2048]{1,0:T(8,128)(2,1)S(1)} %add_convert_fusion.1), channel_id=1, source_target_pairs={{8,0},{16,24},{9,1},{17,25},{10,2},{18,26},{11,3},{19,27},{12,4},{... | collective-permute-start | bytes 4325384 | tf_op jit(solution)/shard_map/ppermute | solution.py:367
  (199 other events, 2183.0 us)
Sparse Core Ops, SparseCore 0:
  22.6 28.2 all-gather.1
where the time goes:
time: 598 us; the launch traced here: 586 us
  waiting for transfers between devices  186 us (31%)
  matrix products  104 us (17%)
  starting transfers between devices  94.5 us (16%)
  Pallas kernels  67.2 us (11%)
  other arithmetic  66.7 us (11%)
  local copies, waits for them, and re-layouts  49.3 us (8%)
  between operations  17.7 us (3%)
    dot_general x61, matrix products, dot(): lax.dot_general(a, b, (dims, ((), ())), preferred_element_type=F32)  104 us
    ppermute x59, waiting for transfers between devices, swap(): return lax.ppermute(values, 'tensor', [(i, i ^ bit) for i in range(n)])  98.6 us
    ppermute x5, waiting for transfers between devices, advance(): self.inward = [(a, lax.ppermute(a, 'dp', [(0, 1), (3, 2)])) for a in arrays]  47.9 us
    ppermute x59, starting transfers between devices, swap(): return lax.ppermute(values, 'tensor', [(i, i ^ bit) for i in range(n)])  35.9 us
    ppermute x5, waiting for transfers between devices, advance(): lax.ppermute(a, 'dp', [(1, 0), (2, 3)])  29.2 us
    pallas_call x2, Pallas kernels, attention_backward(): pl.pallas_call(backward_kernel, grid_spec=pltpu.PrefetchScalarGridSpec(nu...  28.9 us
    unnamed x315, local copies, waits for them, and re-layouts  26.5 us
    ppermute x5, starting transfers between devices, advance(): self.inward = [(a, lax.ppermute(a, 'dp', [(0, 1), (3, 2)])) for a in arrays]  25.5 us
  transfers between devices with their start and end apart: 83, of which 26 were waited for; matrix products, arithmetic and copies ran while one was open for 30% of the time, Pallas kernels for 11%

commit v1 on v0

--- a/solution.py
+++ b/solution.py
@@ -650,7 +650,7 @@
     key_grad = key_grad * own_cos - jnp.roll(key_grad, HEAD // 2, axis=-1) * own_sin
     kv_grad = jnp.concatenate([key_grad, kv_sum[..., HEAD:]], -1).astype(BF16).reshape(flat, 2 * HEAD)
 
-    from_far, far_q, kv_grad = sums.advance([grad_up[1]], (from_far, far_q, kv_grad))
+    far_q = sums.advance([grad_up[1]], far_q)
     grad_in = add_up(near_terms[0], near_core, from_far)
     grad_in = grad_in + dot(kv_grad, kv_weight, ((1,), (1,)))
     kv_portion = dot(norm_in, kv_grad, ((0,), (0,)))

time: 598 us -> 584 us (0.977)
  waiting for transfers between devices: 186 us -> 167 us
  starting transfers between devices: 94.5 us -> 102 us
  other arithmetic: 66.7 us -> 73 us
    ppermute x59, waiting for transfers between devices: 98.6 us -> 74.2 us  [swap(): return lax.ppermute(values, 'tensor', [(i, i ^ bit) for i in range(n)])]
    unnamed x315 -> x301, local copies, waits for them, and re-layouts: 26.5 us -> 26.6 us
  transfers between devices with their start and end apart: 83 -> 83, of which waited for: 26 -> 26; matrix products, arithmetic and copies ran while one was open for 30% -> 31% of each run, Pallas kernels for 11% -> 11%
where the time goes in v1:
time: 584 us; the launch traced here: 573 us
  waiting for transfers between devices  167 us (29%)
  matrix products  105 us (18%)
  starting transfers between devices  102 us (17%)
  other arithmetic  73 us (12%)
  Pallas kernels  61.8 us (11%)
  local copies, waits for them, and re-layouts  47.3 us (8%)
  between operations  17.5 us (3%)
    dot_general x61, matrix products, dot(): lax.dot_general(a, b, (dims, ((), ())), preferred_element_type=F32)  105 us
    ppermute x59, waiting for transfers between devices, swap(): return lax.ppermute(values, 'tensor', [(i, i ^ bit) for i in range(n)])  74.2 us
    ppermute x5, waiting for transfers between devices, advance(): self.inward = [(a, lax.ppermute(a, 'dp', [(0, 1), (3, 2)])) for a in arrays]  49.7 us
    ppermute x59, starting transfers between devices, swap(): return lax.ppermute(values, 'tensor', [(i, i ^ bit) for i in range(n)])  38.7 us
    ppermute x5, waiting for transfers between devices, advance(): lax.ppermute(a, 'dp', [(1, 0), (2, 3)])  29.7 us
    ppermute x5, starting transfers between devices, advance(): self.inward = [(a, lax.ppermute(a, 'dp', [(0, 1), (3, 2)])) for a in arrays]  28.3 us
    unnamed x301, local copies, waits for them, and re-layouts  26.6 us
    pallas_call x2, Pallas kernels, attention_backward(): pl.pallas_call(backward_kernel, grid_spec=pltpu.PrefetchScalarGridSpec(nu...  25.6 us
  transfers between devices with their start and end apart: 83, of which 26 were waited for; matrix products, arithmetic and copies ran while one was open for 31% of the time, Pallas kernels for 11%

profile of v1, /device:TPU:0, one launch (start us, length us, event | category | flops | bytes accessed | tf_op | source)
XLA Modules:
  0.0 572.9 jit_solution(14492170228625240778)
XLA Ops:
  37.0 18.8 %collective-permute-done.5.refs_1_ = bf16[2048,256]{1,0:T(8,128)(2,1)S(1)} collective-permute-done((bf16[2048,256]{1,0:T(8,128)(2,1)}, bf16[2048,256]{1,0:T(8,128)(2,1)S(1)}, u32[]{:S(2)}, u32[]{:S(2)}) %collective-permute-start.5) | collective-permute-done | bytes 1048608 | tf_op jit(solution)/shard_map/ppermute | solution.py:50
  63.6 7.5 %attention_forward.2 = (bf16[2,256,512]{2,1,0:T(8,128)(2,1)S(1)}, bf16[2,2,512,128]{3,2,1,0:T(8,128)(2,1)S(1)}, f32[2,2,8,512]{3,2,1,0:T(8,128)S(1)}) custom-call(s32[2]{0:T(128)S(1)} %pad_add_fusion.1.place, s32[2]{0:T(128)S(1)} %copy-done.14, bf16[256,2048]{1,0:T(8,128)(2,1)} %bitcast.3.x0_ref, bf16[256,2048]{1,0:T(8,128)(2,1)} %collective-permute-done.3.x1_ref, ...), custom_call_target="tpu_custom_call" | custom-call | flops 8053063680 | bytes 524288 | tf_op jit(solution)/shard_map/attention_forward/pallas_call | solution.py:156
  72.6 7.4 %attention_forward.3 = (bf16[2,256,512]{2,1,0:T(8,128)(2,1)S(1)}, bf16[2,2,512,128]{3,2,1,0:T(8,128)(2,1)S(1)}, f32[2,2,8,512]{3,2,1,0:T(8,128)S(1)}) custom-call(s32[2]{0:T(128)S(1)} %pad_add_fusion.place, s32[2]{0:T(128)S(1)} %copy-done.14, bf16[256,2048]{1,0:T(8,128)(2,1)} %collective-permute-done.1.x0_ref, ...), custom_call_target="tpu_custom_call" | custom-call | flops 8053063680 | bytes 524288 | tf_op jit(solution)/shard_map/attention_forward/pallas_call | solution.py:156
  92.6 15.9 %collective-permute-done.10 = bf16[256,2048]{1,0:T(8,128)(2,1)} collective-permute-done((bf16[256,2048]{1,0:T(8,128)(2,1)}, bf16[256,2048]{1,0:T(8,128)(2,1)}, u32[]{:S(2)}, u32[]{:S(2)}) %collective-permute-start.10) | collective-permute-done | bytes 1048608 | tf_op jit(solution)/shard_map/ppermute | solution.py:50
  159.1 4.6 fusion.170
  195.9 4.8 collective-permute-start.27
  213.1 18.4 %collective-permute-done.27 = bf16[352,2048]{1,0:T(8,128)(2,1)S(1)} collective-permute-done((bf16[352,2048]{1,0:T(8,128)(2,1)S(1)}, bf16[352,2048]{1,0:T(8,128)(2,1)S(1)}, u32[]{:S(2)}, u32[]{:S(2)}) %collective-permute-start.27) | collective-permute-done | bytes 1441824 | tf_op jit(solution)/shard_map/ppermute | solution.py:366
  235.2 7.5 %collective-permute-start.28 = (bf16[352,2048]{1,0:T(8,128)(2,1)}, bf16[352,2048]{1,0:T(8,128)(2,1)}, u32[]{:S(2)}, u32[]{:S(2)}) collective-permute-start(bf16[352,2048]{1,0:T(8,128)(2,1)} %get-tuple-element.294.a_ref), channel_id=1, source_target_pairs={{0,8},{24,16},{1,9},{25,17},{2,10},{26,18},{3,11},{27,19},{4,12},{... | collective-permute-start | bytes 4325384 | tf_op jit(solution)/shard_map/ppermute | solution.py:366
  251.2 6.3 %convolution_convert_fusion.1 = bf16[704,2048]{1,0:T(8,128)(2,1)S(1)} fusion(bf16[2048,704]{0,1:T(8,128)(2,1)S(1)} %constant_dynamic-update-slice_fusion.20, bf16[2048,2048]{1,0:T(8,128)(2,1)S(1)} %constant_dynamic-update-slice_fusion.28), kind=kOutput, calls=%fused_computation.26 | convolution fusion | flops 5907021824 | bytes 14155776 | tf_op jit(solution)/shard_map/dot_general | solution.py:54
  260.3 11.4 %collective-permute-done.28.b_ref = bf16[352,2048]{1,0:T(8,128)(2,1)} collective-permute-done((bf16[352,2048]{1,0:T(8,128)(2,1)}, bf16[352,2048]{1,0:T(8,128)(2,1)}, u32[]{:S(2)}, u32[]{:S(2)}) %collective-permute-start.28) | collective-permute-done | bytes 1441824 | tf_op jit(solution)/shard_map/ppermute | solution.py:366
  283.1 8.5 %convolution_convert_fusion = bf16[704,2048]{1,0:T(8,128)(2,1)S(1)} fusion(bf16[2048,704]{0,1:T(8,128)(2,1)S(1)} %constant_dynamic-update-slice_fusion.36, bf16[2048,2048]{1,0:T(8,128)(2,1)} %copy-done.117), kind=kOutput, calls=%fused_computation.25 | convolution fusion | flops 5907021824 | bytes 14155776 | tf_op jit(solution)/shard_map/dot_general | solution.py:54
  291.6 13.0 %attention_backward.2 = (bf16[2,256,512]{2,1,0:T(8,128)(2,1)}, bf16[2,256,2048]{2,1,0:T(8,128)(2,1)}, f32[2,1024,256]{2,1,0:T(8,128)}) custom-call(s32[2]{0:T(128)} %copy-done.16, s32[2]{0:T(128)} %lengths.7, bf16[256,2048]{1,0:T(8,128)(2,1)} %bitcast.26.g0_ref, bf16[256,2048]{1,0:T(8,128)(2,1)} %collective-permute-done.37.g1_ref, ...), custom_call_target="tpu_custom_call" | custom-call | flops 134217728 | bytes 524288 | tf_op jit(solution)/shard_map/attention_backward/pallas_call | solution.py:241
  326.0 12.6 %attention_backward.3 = (bf16[2,256,512]{2,1,0:T(8,128)(2,1)}, bf16[2,256,2048]{2,1,0:T(8,128)(2,1)}, f32[2,1024,256]{2,1,0:T(8,128)}) custom-call(s32[2]{0:T(128)} %copy-done.15, s32[2]{0:T(128)} %lengths.7, bf16[256,2048]{1,0:T(8,128)(2,1)} %collective-permute-done.40.g0_ref, bf16[256,2048]{1,0:T(8,128)(2,1)} %collective-permute-done.43.g1_ref, ...), custom_call_target="tpu_custom_call" | custom-call | flops 134217728 | bytes 524288 | tf_op jit(solution)/shard_map/attention_backward/pallas_call | solution.py:241
  341.2 9.9 %collective-permute-done.41.b_ref = bf16[352,2048]{1,0:T(8,128)(2,1)} collective-permute-done((bf16[352,2048]{1,0:T(8,128)(2,1)}, bf16[352,2048]{1,0:T(8,128)(2,1)}, u32[]{:S(2)}, u32[]{:S(2)}) %collective-permute-start.41) | collective-permute-done | bytes 1441824 | tf_op jit(solution)/shard_map/ppermute | solution.py:359
  365.5 4.7 fusion.19
  402.2 6.0 %fusion.16 = bf16[512,2048]{1,0:T(8,128)(2,1)} fusion(bf16[256,2048]{1,0:T(8,128)(2,1)} %collective-permute-done.2.x1_ref, bf16[256,2048]{1,0:T(8,128)(2,1)} %collective-permute-done.1.x0_ref, bf16[256,2048]{1,0:T(8,128)(2,1)} %collective-permute-done.3.x1_ref, bf16[256,2048]{1,0:T(8,128)(2,1)} %bitcast.3.x0_ref, ...), kind=kOutput, calls=%fused_computation.27 | convolution fusion | flops 2169503744 | bytes 7340032 | tf_op jit(solution)/shard_map/dot_general | solution.py:54
  418.0 6.4 %collective-permute-done.54 = bf16[2,272,256]{2,1,0:T(8,128)(2,1)S(1)} collective-permute-done((bf16[2,272,256]{2,1,0:T(8,128)(2,1)S(1)}, bf16[2,272,256]{2,1,0:T(8,128)(2,1)S(1)}, u32[]{:S(2)}, u32[]{:S(2)}) %collective-permute-start.54) | collective-permute-done | bytes 278560 | tf_op jit(solution)/shard_map/ppermute | solution.py:50
  438.0 7.3 %collective-permute-start.67 = (bf16[256,2048]{1,0:T(8,128)(2,1)S(1)}, bf16[256,2048]{1,0:T(8,128)(2,1)S(1)}, u32[]{:S(2)}, u32[]{:S(2)}) collective-permute-start(bf16[256,2048]{1,0:T(8,128)(2,1)S(1)} %add_convert_fusion.12), channel_id=1, source_target_pairs={{0,8},{24,16},{1,9},{25,17},{2,10},{26,18},{3,11},{27,19},{4,12},{... | collective-permute-start | bytes 3145736 | tf_op jit(solution)/shard_map/ppermute | solution.py:366
  459.9 8.5 %collective-permute-done.68 = bf16[272,256]{1,0:T(8,128)(2,1)S(1)} collective-permute-done((bf16[272,256]{1,0:T(8,128)(2,1)S(1)}, bf16[272,256]{1,0:T(8,128)(2,1)S(1)}, u32[]{:S(2)}, u32[]{:S(2)}) %collective-permute-start.68) | collective-permute-done | bytes 139296 | tf_op jit(solution)/shard_map/ppermute | solution.py:366
  473.9 5.8 %collective-permute-done.64 = bf16[128,2048]{1,0:T(8,128)(2,1)S(1)} collective-permute-done((bf16[128,2048]{1,0:T(8,128)(2,1)S(1)}, bf16[128,2048]{1,0:T(8,128)(2,1)S(1)}, u32[]{:S(2)}, u32[]{:S(2)}) %collective-permute-start.64) | collective-permute-done | bytes 524320 | tf_op jit(solution)/shard_map/ppermute | solution.py:50
  480.7 6.9 %collective-permute-start.71 = (bf16[256,2048]{1,0:T(8,128)(2,1)S(1)}, bf16[256,2048]{1,0:T(8,128)(2,1)S(1)}, u32[]{:S(2)}, u32[]{:S(2)}) collective-permute-start(bf16[256,2048]{1,0:T(8,128)(2,1)S(1)} %add_convert_fusion.9), channel_id=1, source_target_pairs={{0,8},{24,16},{1,9},{25,17},{2,10},{26,18},{3,11},{27,19},{4,12},{... | collective-permute-start | bytes 3145736 | tf_op jit(solution)/shard_map/ppermute | solution.py:366
  493.9 11.4 %collective-permute-done.71 = bf16[256,2048]{1,0:T(8,128)(2,1)S(1)} collective-permute-done((bf16[256,2048]{1,0:T(8,128)(2,1)S(1)}, bf16[256,2048]{1,0:T(8,128)(2,1)S(1)}, u32[]{:S(2)}, u32[]{:S(2)}) %collective-permute-start.71) | collective-permute-done | bytes 1048608 | tf_op jit(solution)/shard_map/ppermute | solution.py:366
  509.2 4.6 collective-permute-done.77
  537.6 23.5 %collective-permute-done.81 = bf16[256,2048]{1,0:T(8,128)(2,1)S(1)} collective-permute-done((bf16[256,2048]{1,0:T(8,128)(2,1)S(1)}, bf16[256,2048]{1,0:T(8,128)(2,1)S(1)}, u32[]{:S(2)}, u32[]{:S(2)}) %collective-permute-start.81) | collective-permute-done | bytes 1048608 | tf_op jit(solution)/shard_map/ppermute | solution.py:367
  (665 shorter events, 323.5 us)
Async XLA Ops:
  7.2 53.4 %all-gather.2.cloned.1.call-start = ((), (), s32[]{:S(2)}) async-start(), calls=%async_computation | async-start | bytes 1179648 | tf_op jit(solution)/shard_map/all_gather | solution.py:518
  12.7 47.9 %collective-permute-start.3 = (bf16[256,2048]{1,0:T(8,128)(2,1)}, bf16[256,2048]{1,0:T(8,128)(2,1)}, u32[]{:S(2)}, u32[]{:S(2)}) collective-permute-start(bf16[256,2048]{1,0:T(8,128)(2,1)} %bitcast.3.x0_ref), channel_id=1, source_target_pairs={{0,1},{1,0},{2,3},{3,2},{4,5},{5,4},{6,7},{7,6},{8,9},{9,8},{10,11... | collective-permute-start | bytes 3145736 | tf_op jit(solution)/shard_map/ppermute | solution.py:50
  13.2 43.7 %collective-permute-start.1 = (bf16[256,2048]{1,0:T(8,128)(2,1)}, bf16[256,2048]{1,0:T(8,128)(2,1)}, u32[]{:S(2)}, u32[]{:S(2)}) collective-permute-start(bf16[256,2048]{1,0:T(8,128)(2,1)} %bitcast.3.x0_ref), channel_id=1, source_target_pairs={{0,4},{1,5},{2,6},{3,7},{4,0},{5,1},{6,2},{7,3},{8,12},{9,13},{10,... | collective-permute-start | bytes 3145736 | tf_op jit(solution)/shard_map/ppermute | solution.py:50
  26.9 53.1 %collective-permute-start = (bf16[256,2048]{1,0:T(8,128)(2,1)}, bf16[256,2048]{1,0:T(8,128)(2,1)}, u32[]{:S(2)}, u32[]{:S(2)}) collective-permute-start(bf16[256,2048]{1,0:T(8,128)(2,1)} %param.18), channel_id=1, source_target_pairs={{0,2},{1,3},{2,0},{3,1},{4,6},{5,7},{6,4},{7,5},{8,10},{9,11},{10,... | collective-permute-start | bytes 3145736 | tf_op jit(solution)/shard_map/ppermute | solution.py:50
  34.9 45.1 %collective-permute-start.6 = (bf16[256,2048]{1,0:T(8,128)(2,1)}, bf16[256,2048]{1,0:T(8,128)(2,1)}, u32[]{:S(2)}, u32[]{:S(2)}) collective-permute-start(bf16[256,2048]{1,0:T(8,128)(2,1)} %bitcast.6), channel_id=1, source_target_pairs={{0,4},{1,5},{2,6},{3,7},{4,0},{5,1},{6,2},{7,3},{8,12},{9,13},{10,... | collective-permute-start | bytes 3145736 | tf_op jit(solution)/shard_map/ppermute | solution.py:50
  130.5 33.1 %collective-permute-start.18 = (bf16[128,2048]{1,0:T(8,128)(2,1)S(1)}, bf16[128,2048]{1,0:T(8,128)(2,1)S(1)}, u32[]{:S(2)}, u32[]{:S(2)}) collective-permute-start(bf16[128,2048]{1,0:T(8,128)(2,1)S(1)} %slice.258), channel_id=1, source_target_pairs={{0,4},{1,5},{2,6},{3,7},{4,0},{5,1},{6,2},{7,3},{8,12},{9,13},{10,... | collective-permute-start | bytes 1572872 | tf_op jit(solution)/shard_map/ppermute | solution.py:50
  195.9 35.7 %collective-permute-start.27 = (bf16[352,2048]{1,0:T(8,128)(2,1)S(1)}, bf16[352,2048]{1,0:T(8,128)(2,1)S(1)}, u32[]{:S(2)}, u32[]{:S(2)}) collective-permute-start(bf16[352,2048]{1,0:T(8,128)(2,1)S(1)} %get-tuple-element.272), channel_id=1, source_target_pairs={{0,8},{24,16},{1,9},{25,17},{2,10},{26,18},{3,11},{27,19},{4,12},{... | collective-permute-start | bytes 4325384 | tf_op jit(solution)/shard_map/ppermute | solution.py:366
  204.8 41.9 %collective-permute-start.30 = (bf16[256,2048]{1,0:T(8,128)(2,1)S(1)}, bf16[256,2048]{1,0:T(8,128)(2,1)S(1)}, u32[]{:S(2)}, u32[]{:S(2)}) collective-permute-start(bf16[256,2048]{1,0:T(8,128)(2,1)S(1)} %fusion.28), channel_id=1, source_target_pairs={{0,1},{1,0},{2,3},{3,2},{4,5},{5,4},{6,7},{7,6},{8,9},{9,8},{10,11... | collective-permute-start | bytes 3145736 | tf_op jit(solution)/shard_map/ppermute | solution.py:50
  206.0 40.8 %collective-permute-start.33 = (bf16[256,2048]{1,0:T(8,128)(2,1)S(1)}, bf16[256,2048]{1,0:T(8,128)(2,1)S(1)}, u32[]{:S(2)}, u32[]{:S(2)}) collective-permute-start(bf16[256,2048]{1,0:T(8,128)(2,1)S(1)} %pad_maximum_fusion.1), channel_id=1, source_target_pairs={{0,2},{1,3},{2,0},{3,1},{4,6},{5,7},{6,4},{7,5},{8,10},{9,11},{10,... | collective-permute-start | bytes 3145736 | tf_op jit(solution)/shard_map/ppermute | solution.py:50
  210.3 36.5 %collective-permute-start.36 = (bf16[256,2048]{1,0:T(8,128)(2,1)S(1)}, bf16[256,2048]{1,0:T(8,128)(2,1)S(1)}, u32[]{:S(2)}, u32[]{:S(2)}) collective-permute-start(bf16[256,2048]{1,0:T(8,128)(2,1)S(1)} %pad_maximum_fusion.2), channel_id=1, source_target_pairs={{0,4},{1,5},{2,6},{3,7},{4,0},{5,1},{6,2},{7,3},{8,12},{9,13},{10,... | collective-permute-start | bytes 3145736 | tf_op jit(solution)/shard_map/ppermute | solution.py:50
  235.2 36.5 %collective-permute-start.28 = (bf16[352,2048]{1,0:T(8,128)(2,1)}, bf16[352,2048]{1,0:T(8,128)(2,1)}, u32[]{:S(2)}, u32[]{:S(2)}) collective-permute-start(bf16[352,2048]{1,0:T(8,128)(2,1)} %get-tuple-element.294.a_ref), channel_id=1, source_target_pairs={{0,8},{24,16},{1,9},{25,17},{2,10},{26,18},{3,11},{27,19},{4,12},{... | collective-permute-start | bytes 4325384 | tf_op jit(solution)/shard_map/ppermute | solution.py:366
  259.5 47.1 %collective-permute-start.40 = (bf16[256,2048]{1,0:T(8,128)(2,1)}, bf16[256,2048]{1,0:T(8,128)(2,1)}, u32[]{:S(2)}, u32[]{:S(2)}) collective-permute-start(bf16[256,2048]{1,0:T(8,128)(2,1)} %bitcast.26.g0_ref), channel_id=1, source_target_pairs={{0,4},{1,5},{2,6},{3,7},{4,0},{5,1},{6,2},{7,3},{8,12},{9,13},{10,... | collective-permute-start | bytes 3145736 | tf_op jit(solution)/shard_map/ppermute | solution.py:50
  276.2 33.4 %collective-permute-start.38 = (bf16[352,2048]{1,0:T(8,128)(2,1)}, bf16[352,2048]{1,0:T(8,128)(2,1)}, u32[]{:S(2)}, u32[]{:S(2)}) collective-permute-start(bf16[352,2048]{1,0:T(8,128)(2,1)} %get-tuple-element.394), channel_id=1, source_target_pairs={{0,8},{8,0},{16,24},{24,16},{1,9},{9,1},{17,25},{25,17},{2,10},{10... | collective-permute-start | bytes 4325384 | tf_op jit(solution)/shard_map/ppermute | solution.py:359
  314.0 37.1 %collective-permute-start.41 = (bf16[352,2048]{1,0:T(8,128)(2,1)}, bf16[352,2048]{1,0:T(8,128)(2,1)}, u32[]{:S(2)}, u32[]{:S(2)}) collective-permute-start(bf16[352,2048]{1,0:T(8,128)(2,1)} %get-tuple-element.396), channel_id=1, source_target_pairs={{0,8},{8,0},{16,24},{24,16},{1,9},{9,1},{17,25},{25,17},{2,10},{10... | collective-permute-start | bytes 4325384 | tf_op jit(solution)/shard_map/ppermute | solution.py:359
  318.6 32.6 %collective-permute-start.42 = (bf16[352,2048]{1,0:T(8,128)(2,1)}, bf16[352,2048]{1,0:T(8,128)(2,1)}, u32[]{:S(2)}, u32[]{:S(2)}) collective-permute-start(bf16[352,2048]{1,0:T(8,128)(2,1)} %get-tuple-element.325.d_ref), channel_id=1, source_target_pairs={{8,16},{16,8},{9,17},{17,9},{10,18},{18,10},{11,19},{19,11},{12,20... | collective-permute-start | bytes 4325384 | tf_op jit(solution)/shard_map/ppermute | solution.py:368
  323.1 85.2 %collective-permute-start.50 = (bf16[256,2048]{1,0:T(8,128)(2,1)}, bf16[256,2048]{1,0:T(8,128)(2,1)}, u32[]{:S(2)}, u32[]{:S(2)}) collective-permute-start(bf16[256,2048]{1,0:T(8,128)(2,1)} %slice_bitcast_fusion.1), channel_id=1, source_target_pairs={{0,1},{1,0},{2,3},{3,2},{4,5},{5,4},{6,7},{7,6},{8,9},{9,8},{10,11... | collective-permute-start | bytes 3145736 | tf_op jit(solution)/shard_map/ppermute | solution.py:50
  340.9 40.7 %collective-permute-start.51 = (bf16[256,2048]{1,0:T(8,128)(2,1)}, bf16[256,2048]{1,0:T(8,128)(2,1)}, u32[]{:S(2)}, u32[]{:S(2)}) collective-permute-start(bf16[256,2048]{1,0:T(8,128)(2,1)} %slice_bitcast_fusion), channel_id=1, source_target_pairs={{0,1},{1,0},{2,3},{3,2},{4,5},{5,4},{6,7},{7,6},{8,9},{9,8},{10,11... | collective-permute-start | bytes 3145736 | tf_op jit(solution)/shard_map/ppermute | solution.py:50
  355.5 38.0 %collective-permute-start.48 = (bf16[352,2048]{1,0:T(8,128)(2,1)}, bf16[352,2048]{1,0:T(8,128)(2,1)}, u32[]{:S(2)}, u32[]{:S(2)}) collective-permute-start(bf16[352,2048]{1,0:T(8,128)(2,1)} %get-tuple-element.386), channel_id=1, source_target_pairs={{0,8},{8,0},{16,24},{24,16},{1,9},{9,1},{17,25},{25,17},{2,10},{10... | collective-permute-start | bytes 4325384 | tf_op jit(solution)/shard_map/ppermute | solution.py:359
  359.9 33.6 %collective-permute-start.49 = (bf16[352,2048]{1,0:T(8,128)(2,1)}, bf16[352,2048]{1,0:T(8,128)(2,1)}, u32[]{:S(2)}, u32[]{:S(2)}) collective-permute-start(bf16[352,2048]{1,0:T(8,128)(2,1)} %get-tuple-element.338.d_ref), channel_id=1, source_target_pairs={{8,16},{16,8},{9,17},{17,9},{10,18},{18,10},{11,19},{19,11},{12,20... | collective-permute-start | bytes 4325384 | tf_op jit(solution)/shard_map/ppermute | solution.py:368
  387.1 38.4 %collective-permute-start.47 = (bf16[256,2048]{1,0:T(8,128)(2,1)}, bf16[256,2048]{1,0:T(8,128)(2,1)}, u32[]{:S(2)}, u32[]{:S(2)}) collective-permute-start(bf16[256,2048]{1,0:T(8,128)(2,1)} %slice.278), channel_id=1, source_target_pairs={{0,2},{1,3},{2,0},{3,1},{4,6},{5,7},{6,4},{7,5},{8,10},{9,11},{10,... | collective-permute-start | bytes 3145736 | tf_op jit(solution)/shard_map/ppermute | solution.py:50
  397.9 33.5 %collective-permute-start.56 = (bf16[352,2048]{1,0:T(8,128)(2,1)}, bf16[352,2048]{1,0:T(8,128)(2,1)}, u32[]{:S(2)}, u32[]{:S(2)}) collective-permute-start(bf16[352,2048]{1,0:T(8,128)(2,1)} %get-tuple-element.388), channel_id=1, source_target_pairs={{0,8},{8,0},{16,24},{24,16},{1,9},{9,1},{17,25},{25,17},{2,10},{10... | collective-permute-start | bytes 4325384 | tf_op jit(solution)/shard_map/ppermute | solution.py:359
  433.4 37.3 %collective-permute-start.70 = (bf16[352,2048]{1,0:T(8,128)(2,1)S(1)}, bf16[352,2048]{1,0:T(8,128)(2,1)S(1)}, u32[]{:S(2)}, u32[]{:S(2)}) collective-permute-start(bf16[352,2048]{1,0:T(8,128)(2,1)S(1)} %add_convert_fusion.2), channel_id=1, source_target_pairs={{8,0},{16,24},{9,1},{17,25},{10,2},{18,26},{11,3},{19,27},{12,4},{... | collective-permute-start | bytes 4325384 | tf_op jit(solution)/shard_map/ppermute | solution.py:367
  437.1 33.6 %collective-permute-start.69 = (bf16[352,2048]{1,0:T(8,128)(2,1)S(1)}, bf16[352,2048]{1,0:T(8,128)(2,1)S(1)}, u32[]{:S(2)}, u32[]{:S(2)}) collective-permute-start(bf16[352,2048]{1,0:T(8,128)(2,1)S(1)} %add_convert_fusion.3), channel_id=1, source_target_pairs={{8,16},{16,8},{9,17},{17,9},{10,18},{18,10},{11,19},{19,11},{12,20... | collective-permute-start | bytes 4325384 | tf_op jit(solution)/shard_map/ppermute | solution.py:368
  471.3 34.0 %collective-permute-start.74 = (bf16[352,2048]{1,0:T(8,128)(2,1)S(1)}, bf16[352,2048]{1,0:T(8,128)(2,1)S(1)}, u32[]{:S(2)}, u32[]{:S(2)}) collective-permute-start(bf16[352,2048]{1,0:T(8,128)(2,1)S(1)} %add_convert_fusion.1), channel_id=1, source_target_pairs={{8,0},{16,24},{9,1},{17,25},{10,2},{18,26},{11,3},{19,27},{12,4},{... | collective-permute-start | bytes 4325384 | tf_op jit(solution)/shard_map/ppermute | solution.py:367
  (192 other events, 1911.2 us)
Sparse Core Ops, SparseCore 0:
  22.6 28.2 all-gather.1
